TPU v7x, 128 devices: a whole 4x4x4 slice. The times are simulated.
128 devices in a mesh: cell: 64 (over z, x, y_lo, core), rcv: 2 (over y_hi).
Axes of the slice: x: 4, y: 4 (y_hi: 2, y_lo: 2; y = y_hi * 2 + y_lo), z: 4, core: 2. Of those that a mesh axis runs over, the one named last changes fastest.
Arguments:
- green: float32 [1024, 131072], P('rcv', 'cell'), may hold values from -0.015625 to 0.015625
- field: float32 [131072, 512], P('cell'), may hold values from -6 to 6
- probe: float32 [4, 131072], P(None, 'cell'), may hold values from -6 to 6
- cov_inv: float32 [1024, 1024], P('rcv'), as said below
Outputs:
- hessian: float32 [4, 131072], P(None, 'cell')
- curvature: float32 [4, 4], replicated
Inputs may be any that keep to these rules, and one draw needn't show every extreme that they name: `cov_inv`: symmetric positive definite.
All inputs are finite; a program needn't handle non-finite values.
Results may differ from a plain program's by a relative error of at most 0.0001.
Values sent between devices are 32-bit elements; how exact they have to be, the bound alone decides.
A program may use at most 128 MiB of HBM per device.

v0:
```python
import jax
import jax.numpy as jnp
from jax import lax
from jax.sharding import PartitionSpec as P


def local(green, field, probe, cov_inv):
    highest_precision = lax.Precision.HIGHEST
    rows_here, cells_here = green.shape
    sources = field.shape[1]
    probes = probe.shape[0]
    receivers = cov_inv.shape[1]
    lifted = (field[:, :, None] * probe.T[:, None, :]).reshape(cells_here, sources * probes)
    partial_value = jnp.dot(
        green, lifted, precision=highest_precision, preferred_element_type=jnp.float32
    )
    measured_data = lax.psum(partial_value, "cell")
    every_row = lax.all_gather(measured_data, "rcv", axis=0, tiled=True)
    whitened_data = jnp.dot(
        cov_inv, every_row, precision=highest_precision, preferred_element_type=jnp.float32
    )
    gram_part = jnp.einsum(
        "dou,dob->ub",
        measured_data.reshape(rows_here, sources, probes),
        whitened_data.reshape(rows_here, sources, probes),
        precision=highest_precision,
    )
    back = lax.dot_general(
        green,
        whitened_data,
        (((0,), (0,)), ((), ())),
        precision=highest_precision,
        preferred_element_type=jnp.float32,
    )
    contrib = jnp.einsum(
        "cs,csp->pc", field, back.reshape(cells_here, sources, probes), precision=highest_precision
    )
    hessian, gram = lax.psum((contrib, gram_part), "rcv")
    curvature = gram / (receivers * sources)
    return (hessian, curvature)


def solution(mesh):
    return jax.shard_map(
        local,
        mesh=mesh,
        in_specs=(P("rcv", "cell"), P("cell", None), P(None, "cell"), P("rcv", None)),
        out_specs=(P(None, "cell"), P()),
        check_vma=False,
    )
```

profile of v0, /device:TPU:0, one launch (start us, length us, event | category | flops | bytes accessed | tf_op | source)
XLA Modules:
  0.0 863.5 jit_solution(6201134448553479928)
XLA Ops:
  7.2 0.0 copy-start
  7.2 0.0 copy-start.6
  7.2 0.0 all-reduce.3.cloned.1.call-start
  7.2 5.6 copy.9
  12.9 0.0 copy-done.6
  12.9 9.9 %broadcast_multiply_fusion = f32[2048,512,4]{0,2,1:T(4,128)} fusion(f32[2048,4]{0,1:T(4,128)S(1)} %bitcast.27, f32[2048,512]{0,1:T(8,128)} %copy.9), kind=kLoop, calls=%fused_computation.2 | loop fusion | flops 4194304 | bytes 21004288 | tf_op jit(solution)/shard_map/mul | solution.py:13
  22.8 19.4 %mul.20 = f32[2048,2048]{0,1:T(8,128)} reshape(f32[2048,512,4]{0,2,1:T(4,128)} %broadcast_multiply_fusion) | data formatting | bytes 33554432 | tf_op jit(solution)/shard_map/mul | solution.py:13
  42.1 31.9 %convolution_bitcast_fusion.1 = f32[512,2048]{0,1:T(8,128)} fusion(f32[2048,2048]{0,1:T(8,128)} %mul.20, f32[512,2048]{1,0:T(8,128)} %param.4), kind=kOutput, calls=%fused_computation.3 | convolution fusion | flops 25769803776 | bytes 25165824 | tf_op jit(solution)/shard_map/dot_general | solution.py:14
  74.0 0.0 all-reduce.3.cloned.1.call-update
  74.1 0.2 all-gather.2.cloned.1.call-start
  74.3 561.0 %all-reduce.3.cloned.1.call-done = f32[512,2048]{0,1:T(8,128)} async-done(((f32[512,2048]{0,1:T(8,128)}), f32[512,2048]{0,1:T(8,128)}) %all-reduce.3.cloned.1.call-update) | async-done | bytes 4194320 | tf_op jit(solution)/shard_map/psum | solution.py:17
  635.3 0.0 all-gather.2.cloned.1.call-update
  635.3 5.2 reshape.20
  640.5 105.4 %all-gather.2.cloned.1.call-done = f32[1024,2048]{0,1:T(8,128)} async-done(((f32[512,2048]{0,1:T(8,128)}), f32[1024,2048]{0,1:T(8,128)}) %all-gather.2.cloned.1.call-update) | async-done | bytes 8388624 | tf_op jit(solution)/shard_map/all_gather | solution.py:18
  745.9 0.0 copy-done
  745.9 0.0 copy-start.5
  745.9 15.8 %fusion = f32[2048,512]{1,0:T(8,128)S(1)} fusion(f32[1024,2048]{0,1:T(8,128)} %all-gather.2.cloned.1.call-done, f32[512,1024]{1,0:T(8,128)S(1)} %copy-done), kind=kOutput, calls=%fused_computation.6 | convolution fusion | flops 12884901888 | bytes 14680064 | tf_op jit(solution)/shard_map/dot_general | solution.py:19
  761.8 0.0 copy-done.5
  761.8 0.0 copy-start.2
  761.8 29.7 %convolution_bitcast_fusion = f32[2048,2048]{0,1:T(8,128)} fusion(f32[2048,512]{1,0:T(8,128)S(1)} %fusion, f32[512,2048]{1,0:T(8,128)S(1)} %copy-done.5), kind=kOutput, calls=%fused_computation.1 | convolution fusion | flops 25769803776 | bytes 25165824 | tf_op jit(solution)/shard_map/dot_general | solution.py:28
  791.5 0.0 copy-done.2
  791.5 5.1 reshape.21
  796.6 19.0 %reshape.19 = f32[2048,512,4]{0,2,1:T(4,128)} reshape(f32[2048,2048]{0,1:T(8,128)} %convolution_bitcast_fusion) | data formatting | bytes 33554432 | tf_op jit(solution)/shard_map/reshape | solution.py:36
  815.6 0.0 copy-start.3
  815.6 0.0 copy-start.4
  815.6 0.0 copy-start.1
  815.6 12.2 %multiply_reduce_fusion = f32[2048,4]{0,1:T(4,128)S(1)} fusion(f32[2048,512,4]{0,2,1:T(4,128)} %reshape.19, f32[2048,512]{0,1:T(8,128)} %copy.9), kind=kLoop, calls=%fused_computation | loop fusion | flops 8380416 | bytes 21004288 | tf_op jit(solution)/shard_map/cs,csp->pc/dot_general | solution.py:35
  827.8 0.0 copy-done.3
  827.8 0.0 copy-done.4
  827.8 19.0 %convolution_bitcast_fusion.2 = f32[4,4]{1,0:T(4,128)S(1)} fusion(f32[512,512,4]{0,2,1:T(4,128)S(1)} %copy-done.3, f32[512,512,4]{0,2,1:T(4,128)S(1)} %copy-done.4), kind=kOutput, calls=%fused_computation.4 | convolution fusion | flops 50331648 | bytes 8388672 | tf_op jit(solution)/shard_map/dou,dob->ub/dot_general | solution.py:22
  846.7 9.3 %all-reduce = (f32[4,2048]{1,0:T(4,128)}, f32[4,4]{1,0:T(4,128)S(1)}) all-reduce(f32[4,2048]{1,0:T(4,128)S(1)} %bitcast.26, f32[4,4]{1,0:T(4,128)S(1)} %convolution_bitcast_fusion.2), channel_id=1, replica_groups=mesh['cell'=64,'rcv'=2] {'rcv'}, use_global_device_ids=true, to_apply=%region_1.0 | all-reduce | flops 8208 | bytes 65664 | tf_op jit(solution)/shard_map/psum | solution.py:38
  856.1 0.6 broadcast_multiply_fusion.1
  856.7 0.0 copy-done.1
Async XLA Ops:
  7.2 738.8 %copy-start = (f32[512,1024]{1,0:T(8,128)S(1)}, f32[512,1024]{1,0:T(8,128)}, u32[]{:S(2)}) copy-start(f32[512,1024]{1,0:T(8,128)} %param.7) | copy-start | bytes 6291460
  7.2 5.7 copy-start.6
  7.2 628.1 %all-reduce.3.cloned.1.call-start = ((), (), s32[]{:S(2)}) async-start(), calls=%async_computation | async-start | bytes 8388608 | tf_op jit(solution)/shard_map/psum | solution.py:17
  74.1 671.9 %all-gather.2.cloned.1.call-start = ((), (), s32[]{:S(2)}) async-start(), calls=%async_computation.1 | async-start | bytes 12582912 | tf_op jit(solution)/shard_map/all_gather | solution.py:18
  745.9 15.8 %copy-start.5 = (f32[512,2048]{1,0:T(8,128)S(1)}, f32[512,2048]{1,0:T(8,128)}, u32[]{:S(2)}) copy-start(f32[512,2048]{1,0:T(8,128)} %param.4) | copy-start | bytes 12582916
  761.8 29.7 %copy-start.2 = (f32[2048,512]{1,0:T(8,128)}, f32[2048,512]{1,0:T(8,128)S(1)}, u32[]{:S(2)}) copy-start(f32[2048,512]{1,0:T(8,128)S(1)} %fusion) | copy-start | bytes 12582916
  815.6 12.2 %copy-start.3 = (f32[512,512,4]{0,2,1:T(4,128)S(1)}, f32[512,512,4]{0,2,1:T(4,128)}, u32[]{:S(2)}) copy-start(f32[512,512,4]{0,2,1:T(4,128)} %reshape.20) | copy-start | bytes 12582916
  815.6 12.2 %copy-start.4 = (f32[512,512,4]{0,2,1:T(4,128)S(1)}, f32[512,512,4]{0,2,1:T(4,128)}, u32[]{:S(2)}) copy-start(f32[512,512,4]{0,2,1:T(4,128)} %reshape.21) | copy-start | bytes 12582916
  815.6 41.1 %copy-start.1 = (f32[512,1024]{1,0:T(8,128)S(1)}, f32[512,1024]{1,0:T(8,128)}, u32[]{:S(2)}) copy-start(f32[512,1024]{1,0:T(8,128)} %param.7) | copy-start | bytes 6291460
Sparse Core Ops, SparseCore 0:
  74.2 561.0 all-reduce.2
  637.1 108.8 all-gather.1
where the time goes:
time: 865 us; the launch traced here: 864 us
  waiting for transfers between devices  666 us (77%)
  matrix products  96.4 us (11%)
  local copies, waits for them, and re-layouts  54.3 us (6%)
  other arithmetic  22.6 us (3%)
  between operations  14.1 us (2%)
  blocking collectives  9.34 us (1%)
    psum x1, waiting for transfers between devices, local(): measured_data = lax.psum(partial_value, 'cell')  561 us
    all_gather x1, waiting for transfers between devices, local(): every_row = lax.all_gather(measured_data, 'rcv', axis=0, tiled=True)  105 us
    dot_general x1, matrix products, local(): jnp.dot(green, lifted, precision=highest_precision, preferred_element_typ...  31.9 us
    dot_general x1, matrix products, local(): lax.dot_general(green, whitened_data, (((0,), (0,)), ((), ())), precision...  29.7 us
    mul x1, local copies, waits for them, and re-layouts, local(): field[:, :, None] * probe.T[:, None, :]  19.4 us
    reshape x1, local copies, waits for them, and re-layouts, local(): back.reshape(cells_here, sources, probes)  19 us
    dot_general x1, matrix products, local(): jnp.einsum('dou,dob->ub', measured_data.reshape(rows_here, sources, probe...  19 us
  transfers between devices with their start and end apart: 2, of which 2 were waited for; matrix products, arithmetic and copies ran while one was open for 1% of the time, Pallas kernels for 0%

commit v1 on v0

v1 whole, which is shorter than its diff:
```python
import functools

import jax
import jax.numpy as jnp
from jax import lax
from jax.experimental import pallas as pl
from jax.experimental.pallas import tpu as pltpu
from jax.sharding import PartitionSpec as P

MESH = pl.DeviceIdType.MESH
F32 = jnp.float32
BF16 = jnp.bfloat16
NP = 4
S = 512
R = 512
C = 2048
KB = 512
NKB = C // KB
NB = 512
NNB = C // NB

ORDER = """F1.0 F0.0 C.0 F1.1 F0.1 C.1 F1.2 A.0 F0.2 C.2 F1.3 A.1 Y.0 F0.3 C.3
A.2 R.0 Y.1 A.3 R.1 Y.2 V.0 U.0 R.2 Y.3 V.1 B0.0 U.1 R.3 G0 V.2 B1.0 U.2 B0.1 V.3 G1 B1.1 U.3 G2 B0.2 G3 B1.2
B0.3 B1.3""".split()


def flip(v, m):
    if m == 0:
        return v
    if m == 1:
        return v + 1 - 2 * lax.rem(v, 2)
    if m == 2:
        return lax.rem(v + 2, 4)
    return 3 - v


def split(a):
    hi = a.astype(BF16)
    return hi, (a - hi.astype(F32)).astype(BF16)


def nt(a, b):
    return lax.dot_general(a, b, (((1,), (1,)), ((), ())), preferred_element_type=F32)


def nn(a, b):
    return lax.dot_general(a, b, (((1,), (0,)), ((), ())), preferred_element_type=F32)


def kernel(order, green, field, probe, cov, h_out, hr_out, g_out,
           graw, fraw, craw, prb, ghi, glo, ft, chi, clo, data, core_in, ring_in, pair_in, own, far, white, hess,
           gram, g8, g4, g2, g1, lsem, ssem, rsem):
    cell = lax.axis_index("cell")
    rcv = lax.axis_index("rcv")
    core = lax.rem(cell, 2)
    yl = lax.rem(cell // 2, 2)
    x = lax.rem(cell // 4, 4)
    z = cell // 16

    def device(m1, m2, my, mc):
        z1, x1 = flip(z, m1), flip(x, m1)
        z2, x2 = flip(z, m2), flip(x, m2)
        zz = z2 + core * (z1 - z2)
        xx = x1 + core * (x2 - x1)
        yy = 1 - yl if my else yl
        cc = 1 - core if mc else core
        return (((zz * 4 + xx) * 2 + yy) * 2 + cc, rcv)

    sibling = device(0, 0, 0, 1)
    other = (cell, 1 - rcv)
    ring = [None] + [device(m, 0, 0, 0) for m in (1, 2, 3)]
    pairs = [None] + [device(0, m // 2, m % 2, 0) for m in range(1, 8)]

    loads = []
    for k in range(NKB):
        cells = pl.ds(k * KB, KB)
        loads.append(pltpu.make_async_copy(field.at[cells, :], fraw.at[cells, :], lsem.at[2 * k]))
        loads.append(pltpu.make_async_copy(green.at[:, cells], graw.at[:, cells], lsem.at[2 * k + 1]))
    load_probe = pltpu.make_async_copy(probe, prb, lsem.at[2 * NKB])
    load_cov = pltpu.make_async_copy(cov, craw, lsem.at[2 * NKB + 1])
    load_probe.start()
    for c in loads:
        c.start()
    load_cov.start()

    barrier = pltpu.get_barrier_semaphore()
    partners = [sibling, other] + ring[1:] + pairs[1:]
    for d in partners:
        pl.semaphore_signal(barrier, inc=1, device_id=d, device_id_type=MESH)

    started = []
    counter = [0]

    def remote(src, dst, dev):
        n = counter[0]
        counter[0] += 1
        c = pltpu.make_async_remote_copy(src_ref=src, dst_ref=dst, send_sem=ssem.at[n], recv_sem=rsem.at[n],
                                         device_id=dev, device_id_type=MESH)
        c.start()
        started.append(c)
        return c

    place1 = [[flip(x if c == 0 else z, a) for a in range(4)] for c in range(2)]
    place2 = [[flip(z if c == 0 else x, a) for a in range(4)] for c in range(2)]
    place_y = [yl, 1 - yl]
    place_c = [core, 1 - core]

    load_probe.wait()
    for k in range(NKB):
        cells = slice(k * KB, (k + 1) * KB)
        loads[2 * k].wait()
        turned = fraw[cells, :].T
        for c in range(2):
            for a1 in range(4):
                for a2 in range(4):
                    for y in range(2):
                        g = ((c * 4 + a1) * 4 + a2) * 2 + y
                        slot = ((place_c[c] * 4 + place1[c][a1]) * 4 + place2[c][a2]) * 2 + place_y[y]
                        ft[pl.ds(pl.multiple_of(slot * 8, 8), 8), cells] = turned[g * 8:(g + 1) * 8, :]
        loads[2 * k + 1].wait()
        ghi[:, cells], glo[:, cells] = split(graw[:, cells])

    waits = {}

    def forward(p, half):
        rows = slice(half * 256, half * 256 + 256)

        def step(k, _):
            cells = pl.ds(pl.multiple_of(k * KB, KB), KB)
            hi, lo = split(ft[rows, cells] * prb[p:p + 1, cells])
            part = nt(hi, ghi[:, cells]) + nt(hi, glo[:, cells]) + nt(lo, ghi[:, cells])

            @pl.when(k == 0)
            def _():
                data[p, rows] = part

            @pl.when(k > 0)
            def _():
                data[p, rows] += part

            return 0

        lax.fori_loop(0, NKB, step, 0)

    def whiten(p):
        waits["R", p].wait_recv()
        total = jnp.zeros((8, R), F32)
        for mine, vals in ((True, own[p]), (False, far[p])):
            hi, lo = split(vals)
            both = jnp.concatenate([hi, lo], axis=0)
            start = pl.multiple_of((rcv if mine else 1 - rcv) * R, R)
            a = nt(both, chi[:, pl.ds(start, R)])
            b = nt(both, clo[:, pl.ds(start, R)])
            total += (a[:8] + a[8:]) + (b[:8] + b[8:])
        white[p, 0:8] = total

    def backward(p, half):
        rows = slice(half * 256, half * 256 + 256)
        hi, lo = split(white[p, rows])

        def step(n, _):
            cells = pl.ds(pl.multiple_of(n * NB, NB), NB)
            g, l = ghi[:, cells], glo[:, cells]
            back = nn(hi, g) + nn(hi, l) + nn(lo, g)
            part = jnp.sum(back * ft[rows, cells], axis=0, keepdims=True)
            if half == 0:
                hess[p, :, cells] = part
            else:
                hess[p, :, cells] += part
            return 0

        lax.fori_loop(0, NNB, step, 0)

    first = [True]
    for word in order:
        op, _, p = word.partition(".")
        p = int(p) if p else 0
        if op == "F1":
            forward(p, 1)
            if first[0]:
                pl.semaphore_wait(barrier, len(partners))
                first[0] = False
            waits["C", p] = [remote(data.at[p, pl.ds(256, 256)], core_in.at[p], sibling)]
        elif op == "F0":
            forward(p, 0)
        elif op == "C":
            waits["C", p][0].wait_recv()
            data[p, 0:256] += core_in[p]
            waits["A", p] = [remote(data.at[p, pl.ds(64 * m, 64)], ring_in.at[p, m - 1], ring[m]) for m in (2, 1, 3)]
        elif op == "A":
            for c in waits["A", p]:
                c.wait_recv()
            data[p, 0:64] = (data[p, 0:64] + ring_in[p, 0]) + (ring_in[p, 1] + ring_in[p, 2])
            waits["Y", p] = [remote(data.at[p, pl.ds(8 * m, 8)], pair_in.at[p, m - 1], pairs[m])
                             for m in (5, 4, 7, 3, 6, 2, 1)]
            if p == 0:
                load_cov.wait()
                chi[...], clo[...] = split(craw[...])
        elif op == "Y":
            for c in waits["Y", p]:
                c.wait_recv()
            total = data[p, 0:8]
            for m in range(7):
                total += pair_in[p, m]
            own[p] = total
            waits["R", p] = remote(own.at[p], far.at[p], other)
        elif op == "R":
            whiten(p)
            waits["V", p] = [remote(white.at[p, pl.ds(0, 8)], white.at[p, pl.ds(8 * m, 8)], pairs[m])
                             for m in (5, 4, 7, 3, 6, 2, 1)]
        elif op == "V":
            for c in waits["V", p]:
                c.wait_recv()
            waits["U", p] = [remote(white.at[p, pl.ds(0, 64)], white.at[p, pl.ds(64 * m, 64)], ring[m])
                             for m in (2, 1, 3)]
        elif op == "U":
            for c in waits["U", p]:
                c.wait_recv()
            waits["S", p] = remote(white.at[p, pl.ds(0, 256)], white.at[p, pl.ds(256, 256)], sibling)
        elif op == "B0":
            backward(p, 0)
        elif op == "B1":
            waits["S", p].wait_recv()
            backward(p, 1)
            waits["H", p] = remote(hess.at[p], hr_out.at[p], other)
        elif op == "G0":
            for a in range(NP):
                for b in range(NP):
                    t = jnp.sum(own[a] * white[b, 0:8], axis=0, keepdims=True)
                    gram[a * NP + b:a * NP + b + 1, :] = (t[:, 0:128] + t[:, 128:256]) + (t[:, 256:384] + t[:, 384:])
            waits["G"] = [remote(gram, g8.at[m - 1], pairs[m]) for m in range(1, 8)]
        elif op == "G1":
            for c in waits["G"]:
                c.wait_recv()
            total = gram[...]
            for m in range(7):
                total += g8[m]
            g1[0] = total
            waits["G"] = [remote(g1.at[0], g4.at[m - 1], ring[m]) for m in (1, 2, 3)]
        elif op == "G2":
            for c in waits["G"]:
                c.wait_recv()
            g1[1] = (g1[0] + g4[0]) + (g4[1] + g4[2])
            waits["G"] = [remote(g1.at[1], g2.at[0], sibling)]
        elif op == "G3":
            waits["G"][0].wait_recv()
            g1[2] = g1[1] + g2[0]
            waits["G"] = [remote(g1.at[2], g2.at[1], other)]
    for p in range(NP):
        if ("H", p) in waits:
            waits["H", p].wait_recv()
        h_out[p] = hess[p]
    waits["G"][0].wait_recv()
    g_out[...] = g1[2] + g2[1]
    for c in started:
        c.wait_send()


def local(green, field, probe, cov):
    any_spec = pl.BlockSpec(memory_space=pl.ANY)
    vmem = pl.BlockSpec(memory_space=pltpu.VMEM)
    n_remote = NP * 24 + 12
    h, hr, g = pl.pallas_call(
        functools.partial(kernel, ORDER),
        name="probes",
        out_shape=(jax.ShapeDtypeStruct((NP, 1, C), F32), jax.ShapeDtypeStruct((NP, 1, C), F32),
                   jax.ShapeDtypeStruct((16, 128), F32)),
        in_specs=[any_spec] * 4,
        out_specs=(vmem, vmem, vmem),
        scratch_shapes=[
            pltpu.VMEM((R, C), F32),
            pltpu.VMEM((C, S), F32),
            pltpu.VMEM((R, 2 * R), F32),
            pltpu.VMEM((NP, C), F32),
            pltpu.VMEM((R, C), BF16),
            pltpu.VMEM((R, C), BF16),
            pltpu.VMEM((S, C), F32),
            pltpu.VMEM((R, 2 * R), BF16),
            pltpu.VMEM((R, 2 * R), BF16),
            pltpu.VMEM((NP, S, R), F32),
            pltpu.VMEM((NP, 256, R), F32),
            pltpu.VMEM((NP, 3, 64, R), F32),
            pltpu.VMEM((NP, 7, 8, R), F32),
            pltpu.VMEM((NP, 8, R), F32),
            pltpu.VMEM((NP, 8, R), F32),
            pltpu.VMEM((NP, S, R), F32),
            pltpu.VMEM((NP, 1, C), F32),
            pltpu.VMEM((16, 128), F32),
            pltpu.VMEM((7, 16, 128), F32),
            pltpu.VMEM((3, 16, 128), F32),
            pltpu.VMEM((2, 16, 128), F32),
            pltpu.VMEM((3, 16, 128), F32),
            pltpu.SemaphoreType.DMA((2 * NKB + 2,)),
            pltpu.SemaphoreType.DMA((n_remote,)),
            pltpu.SemaphoreType.DMA((n_remote,)),
        ],
        compiler_params=pltpu.CompilerParams(collective_id=0, has_side_effects=True, vmem_limit_bytes=56 * 2 ** 20),
        cost_estimate=pl.CostEstimate(flops=6 * 2 * R * C * S * NP, bytes_accessed=10 * 2 ** 20, transcendentals=0),
    )(green, field, probe, cov)
    hessian = (h + hr).reshape(NP, C)
    curvature = jnp.sum(g, axis=1).reshape(NP, NP) / (1024 * S)
    return hessian, curvature


def solution(mesh):
    return jax.shard_map(
        local,
        mesh=mesh,
        in_specs=(P("rcv", "cell"), P("cell", None), P(None, "cell"), P("rcv", None)),
        out_specs=(P(None, "cell"), P()),
        check_vma=False,
    )
```

time: 865 us -> 85.3 us (0.10)
  waiting for transfers between devices: 666 us -> 0 us
  matrix products: 96.4 us -> 0 us
  Pallas kernels: 0 us -> 81.5 us
  local copies, waits for them, and re-layouts: 54.3 us -> 1.29 us
  other arithmetic: 22.6 us -> 1.63 us
  between operations: 14.1 us -> 0.64 us
  blocking collectives: 9.34 us -> 0 us
    psum x1 -> x0, waiting for transfers between devices: 561 us -> none  [local(): measured_data = lax.psum(partial_value, 'cell')]
    all_gather x1 -> x0, waiting for transfers between devices: 105 us -> none  [local(): every_row = lax.all_gather(measured_data, 'rcv', axis=0, tiled=True)]
    dot_general x4 -> x0, matrix products: 96.4 us -> none  [the longest x1 31.9 us: local(): jnp.dot(green, lifted, precision=highest_precision, preferred_element_typ...]
    pallas_call x0 -> x1, Pallas kernels: none -> 81.5 us  [local(): pl.pallas_call(functools.partial(kernel, ORDER), name='probes', out_shape...]
    reshape x3 -> x0, local copies, waits for them, and re-layouts: 29.3 us -> none  [the longest x1 19 us: local(): back.reshape(cells_here, sources, probes)]
    mul x1 -> x0, local copies, waits for them, and re-layouts: 19.4 us -> none  [local(): field[:, :, None] * probe.T[:, None, :]]
    dot_general x1 -> x0, other arithmetic: 12.2 us -> none  [local(): jnp.einsum('cs,csp->pc', field, back.reshape(cells_here, sources, probes)...]
    mul x1 -> x0, other arithmetic: 9.89 us -> none  [local(): field[:, :, None] * probe.T[:, None, :]]
  transfers between devices with their start and end apart: 2 -> 0, of which waited for: 2 -> 0; matrix products, arithmetic and copies ran while one was open for 1% -> 0% of each run, Pallas kernels for 0% -> 0%
where the time goes in v1:
time: 85.3 us; the launch traced here: 85 us
  Pallas kernels  81.5 us (96%)
  other arithmetic  1.63 us (2%)
  local copies, waits for them, and re-layouts  1.29 us (2%)
    pallas_call x1, Pallas kernels, local(): pl.pallas_call(functools.partial(kernel, ORDER), name='probes', out_shape...  81.5 us

profile of v1, /device:TPU:0, one launch (start us, length us, event | category | flops | bytes accessed | tf_op | source)
XLA Modules:
  0.0 85.0 jit_solution(11407901756749170142)
XLA Ops:
  0.6 81.5 %probes.1 = (f32[4,1,2048]{2,1,0:T(1,128)}, f32[4,1,2048]{2,1,0:T(1,128)}, f32[16,128]{1,0:T(8,128)}) custom-call(f32[512,2048]{1,0:T(8,128)} %green.1, f32[2048,512]{1,0:T(8,128)} %field.1, f32[4,2048]{1,0:T(4,128)} %probe.1, f32[512,1024]{1,0:T(8,128)} %cov.1), custom_call_target="tpu_custom_call" | custom-call | flops 25769803776 | bytes 10485760 | tf_op jit(solution)/shard_map/probes/pallas_call | solution.py:263
  82.1 0.8 add.3
  82.9 0.6 copy.8
  83.6 0.8 reduce_sum.9
  84.4 0.7 div.6
  (1 shorter events, 0.0 us)

commit v2 on v1

--- a/solution.py
+++ b/solution.py
@@ -19,9 +19,13 @@
 NB = 512
 NNB = C // NB
 
-ORDER = """F1.0 F0.0 C.0 F1.1 F0.1 C.1 F1.2 A.0 F0.2 C.2 F1.3 A.1 Y.0 F0.3 C.3
-A.2 R.0 Y.1 A.3 R.1 Y.2 V.0 U.0 R.2 Y.3 V.1 B0.0 U.1 R.3 G0 V.2 B1.0 U.2 B0.1 V.3 G1 B1.1 U.3 G2 B0.2 G3 B1.2
-B0.3 B1.3""".split()
+ORDER = [
+    "F1a.0", "F1b.0", "F0a.0", "F0b.0", "F1a.1", "C.0", "F1b.1", "F0a.1", "F0b.1", "F1a.2", "C.1", "F1b.2",
+    "F0a.2", "F0b.2", "A.0", "F1a.3", "C.2", "F1b.3", "F0a.3", "F0b.3", "A.1", "C.3", "R.0", "A.2", "R.1",
+    "A.3", "V.0", "R.2", "V.1", "U.0", "B0a.0", "R.3", "V.2", "B0b.0", "G0", "U.1", "B1a.0", "B1b.0",
+    "B0a.1", "V.3", "B0b.1", "B1a.1", "U.2", "B1b.1", "G1", "B0a.2", "B0b.2", "B1a.2", "U.3", "B1b.2",
+    "B0a.3", "B0b.3", "G2", "B1a.3", "B1b.3", "G3",
+]
 
 
 def flip(v, m):
@@ -47,8 +51,8 @@
     return lax.dot_general(a, b, (((1,), (0,)), ((), ())), preferred_element_type=F32)
 
 
-def kernel(order, green, field, probe, cov, h_out, hr_out, g_out,
-           graw, fraw, craw, prb, ghi, glo, ft, chi, clo, data, core_in, ring_in, pair_in, own, far, white, hess,
+def kernel(order, green, field, probe, cov, h_out, g_out,
+           graw, fraw, craw, prb, ghi, glo, ft, chi, clo, data, core_in, ring_in, pair_in, own, white, hess, hess_in,
            gram, g8, g4, g2, g1, lsem, ssem, rsem):
     cell = lax.axis_index("cell")
     rcv = lax.axis_index("rcv")
@@ -57,17 +61,18 @@
     x = lax.rem(cell // 4, 4)
     z = cell // 16
 
-    def device(m1, m2, my, mc):
+    def device(m1, m2, my, mc, mr=0):
         z1, x1 = flip(z, m1), flip(x, m1)
         z2, x2 = flip(z, m2), flip(x, m2)
         zz = z2 + core * (z1 - z2)
         xx = x1 + core * (x2 - x1)
         yy = 1 - yl if my else yl
         cc = 1 - core if mc else core
-        return (((zz * 4 + xx) * 2 + yy) * 2 + cc, rcv)
+        return (((zz * 4 + xx) * 2 + yy) * 2 + cc, 1 - rcv if mr else rcv)
 
     sibling = device(0, 0, 0, 1)
-    other = (cell, 1 - rcv)
+    other = device(0, 0, 0, 0, 1)
+    facing = [device(0, m // 2, m % 2, 0, 1) for m in range(8)]
     ring = [None] + [device(m, 0, 0, 0) for m in (1, 2, 3)]
     pairs = [None] + [device(0, m // 2, m % 2, 0) for m in range(1, 8)]
 
@@ -84,7 +89,7 @@
     load_cov.start()
 
     barrier = pltpu.get_barrier_semaphore()
-    partners = [sibling, other] + ring[1:] + pairs[1:]
+    partners = [sibling] + facing + ring[1:] + pairs[1:]
     for d in partners:
         pl.semaphore_signal(barrier, inc=1, device_id=d, device_id_type=MESH)
 
@@ -122,30 +127,27 @@
 
     waits = {}
 
-    def forward(p, half):
+    def forward(p, half, part_at):
         rows = slice(half * 256, half * 256 + 256)
 
-        def step(k, _):
-            cells = pl.ds(pl.multiple_of(k * KB, KB), KB)
+        total = data[p, rows] if part_at else None
+        for k in range(part_at * NKB // 2, (part_at + 1) * NKB // 2):
+            cells = slice(k * KB, (k + 1) * KB)
             hi, lo = split(ft[rows, cells] * prb[p:p + 1, cells])
             part = nt(hi, ghi[:, cells]) + nt(hi, glo[:, cells]) + nt(lo, ghi[:, cells])
-
-            @pl.when(k == 0)
-            def _():
-                data[p, rows] = part
-
-            @pl.when(k > 0)
-            def _():
-                data[p, rows] += part
-
-            return 0
-
-        lax.fori_loop(0, NKB, step, 0)
+            total = part if total is None else total + part
+        data[p, rows] = total
 
     def whiten(p):
-        waits["R", p].wait_recv()
+        for c in waits["R", p]:
+            c.wait_recv()
+        near, away = data[p, 0:8], pair_in[p, 7]
+        for m in range(7):
+            near += pair_in[p, m]
+            away += pair_in[p, 8 + m]
+        own[p] = near
         total = jnp.zeros((8, R), F32)
-        for mine, vals in ((True, own[p]), (False, far[p])):
+        for mine, vals in ((True, near), (False, away)):
             hi, lo = split(vals)
             both = jnp.concatenate([hi, lo], axis=0)
             start = pl.multiple_of((rcv if mine else 1 - rcv) * R, R)
@@ -154,12 +156,12 @@
             total += (a[:8] + a[8:]) + (b[:8] + b[8:])
         white[p, 0:8] = total
 
-    def backward(p, half):
+    def backward(p, half, part_at):
         rows = slice(half * 256, half * 256 + 256)
         hi, lo = split(white[p, rows])
 
-        def step(n, _):
-            cells = pl.ds(pl.multiple_of(n * NB, NB), NB)
+        for n in range(part_at * NNB // 2, (part_at + 1) * NNB // 2):
+            cells = slice(n * NB, (n + 1) * NB)
             g, l = ghi[:, cells], glo[:, cells]
             back = nn(hi, g) + nn(hi, l) + nn(lo, g)
             part = jnp.sum(back * ft[rows, cells], axis=0, keepdims=True)
@@ -167,22 +169,23 @@
                 hess[p, :, cells] = part
             else:
                 hess[p, :, cells] += part
-            return 0
-
-        lax.fori_loop(0, NNB, step, 0)
 
     first = [True]
     for word in order:
         op, _, p = word.partition(".")
         p = int(p) if p else 0
-        if op == "F1":
-            forward(p, 1)
+        if op == "F1a":
+            forward(p, 1, 0)
+        elif op == "F1b":
+            forward(p, 1, 1)
             if first[0]:
                 pl.semaphore_wait(barrier, len(partners))
                 first[0] = False
             waits["C", p] = [remote(data.at[p, pl.ds(256, 256)], core_in.at[p], sibling)]
-        elif op == "F0":
-            forward(p, 0)
+        elif op == "F0a":
+            forward(p, 0, 0)
+        elif op == "F0b":
+            forward(p, 0, 1)
         elif op == "C":
             waits["C", p][0].wait_recv()
             data[p, 0:256] += core_in[p]
@@ -191,19 +194,12 @@
             for c in waits["A", p]:
                 c.wait_recv()
             data[p, 0:64] = (data[p, 0:64] + ring_in[p, 0]) + (ring_in[p, 1] + ring_in[p, 2])
-            waits["Y", p] = [remote(data.at[p, pl.ds(8 * m, 8)], pair_in.at[p, m - 1], pairs[m])
-                             for m in (5, 4, 7, 3, 6, 2, 1)]
+            waits["R", p] = [remote(data.at[p, pl.ds(8 * m, 8)], pair_in.at[p, n], dev) for m, n, dev in
+                             [(m, 7 + m, facing[m]) for m in (5, 4, 7, 3, 6, 2, 1, 0)]
+                             + [(m, m - 1, pairs[m]) for m in (5, 4, 7, 3, 6, 2, 1)]]
             if p == 0:
                 load_cov.wait()
                 chi[...], clo[...] = split(craw[...])
-        elif op == "Y":
-            for c in waits["Y", p]:
-                c.wait_recv()
-            total = data[p, 0:8]
-            for m in range(7):
-                total += pair_in[p, m]
-            own[p] = total
-            waits["R", p] = remote(own.at[p], far.at[p], other)
         elif op == "R":
             whiten(p)
             waits["V", p] = [remote(white.at[p, pl.ds(0, 8)], white.at[p, pl.ds(8 * m, 8)], pairs[m])
@@ -217,12 +213,16 @@
             for c in waits["U", p]:
                 c.wait_recv()
             waits["S", p] = remote(white.at[p, pl.ds(0, 256)], white.at[p, pl.ds(256, 256)], sibling)
-        elif op == "B0":
-            backward(p, 0)
-        elif op == "B1":
+        elif op == "B0a":
+            backward(p, 0, 0)
+        elif op == "B0b":
+            backward(p, 0, 1)
+        elif op == "B1a":
             waits["S", p].wait_recv()
-            backward(p, 1)
-            waits["H", p] = remote(hess.at[p], hr_out.at[p], other)
+            backward(p, 1, 0)
+        elif op == "B1b":
+            backward(p, 1, 1)
+            waits["H", p] = remote(hess.at[p], hess_in.at[p], other)
         elif op == "G0":
             for a in range(NP):
                 for b in range(NP):
@@ -247,11 +247,13 @@
             g1[2] = g1[1] + g2[0]
             waits["G"] = [remote(g1.at[2], g2.at[1], other)]
     for p in range(NP):
-        if ("H", p) in waits:
-            waits["H", p].wait_recv()
-        h_out[p] = hess[p]
+        waits["H", p].wait_recv()
+        h_out[p:p + 1, :] = hess[p] + hess_in[p]
     waits["G"][0].wait_recv()
-    g_out[...] = g1[2] + g2[1]
+    sums = jnp.sum(g1[2] + g2[1], axis=1, keepdims=True) * (1.0 / (2 * R * S))
+    for a in range(NP):
+        for b in range(NP):
+            g_out[a:a + 1, b:b + 1] = sums[a * NP + b:a * NP + b + 1, :]
     for c in started:
         c.wait_send()
 
@@ -259,14 +261,13 @@
 def local(green, field, probe, cov):
     any_spec = pl.BlockSpec(memory_space=pl.ANY)
     vmem = pl.BlockSpec(memory_space=pltpu.VMEM)
-    n_remote = NP * 24 + 12
-    h, hr, g = pl.pallas_call(
+    n_remote = NP * 32 + 12
+    return pl.pallas_call(
         functools.partial(kernel, ORDER),
         name="probes",
-        out_shape=(jax.ShapeDtypeStruct((NP, 1, C), F32), jax.ShapeDtypeStruct((NP, 1, C), F32),
-                   jax.ShapeDtypeStruct((16, 128), F32)),
+        out_shape=(jax.ShapeDtypeStruct((NP, C), F32), jax.ShapeDtypeStruct((NP, NP), F32)),
         in_specs=[any_spec] * 4,
-        out_specs=(vmem, vmem, vmem),
+        out_specs=(vmem, vmem),
         scratch_shapes=[
             pltpu.VMEM((R, C), F32),
             pltpu.VMEM((C, S), F32),
@@ -280,10 +281,10 @@
             pltpu.VMEM((NP, S, R), F32),
             pltpu.VMEM((NP, 256, R), F32),
             pltpu.VMEM((NP, 3, 64, R), F32),
-            pltpu.VMEM((NP, 7, 8, R), F32),
-            pltpu.VMEM((NP, 8, R), F32),
+            pltpu.VMEM((NP, 15, 8, R), F32),
             pltpu.VMEM((NP, 8, R), F32),
             pltpu.VMEM((NP, S, R), F32),
+            pltpu.VMEM((NP, 1, C), F32),
             pltpu.VMEM((NP, 1, C), F32),
             pltpu.VMEM((16, 128), F32),
             pltpu.VMEM((7, 16, 128), F32),
@@ -297,9 +298,6 @@
         compiler_params=pltpu.CompilerParams(collective_id=0, has_side_effects=True, vmem_limit_bytes=56 * 2 ** 20),
         cost_estimate=pl.CostEstimate(flops=6 * 2 * R * C * S * NP, bytes_accessed=10 * 2 ** 20, transcendentals=0),
     )(green, field, probe, cov)
-    hessian = (h + hr).reshape(NP, C)
-    curvature = jnp.sum(g, axis=1).reshape(NP, NP) / (1024 * S)
-    return hessian, curvature
 
 
 def solution(mesh):

time: 85.3 us -> 68.4 us (0.80)
  Pallas kernels: 81.5 us -> 64.9 us
  other arithmetic: 1.63 us -> 0 us
  local copies, waits for them, and re-layouts: 1.29 us -> 2.62 us
    pallas_call x1, Pallas kernels: 81.5 us -> 64.9 us  [local(): pl.pallas_call(functools.partial(kernel, ORDER), name='probes', out_shape...]
    unnamed x1 -> x2, local copies, waits for them, and re-layouts: 0.63 us -> 2.62 us
where the time goes in v2:
time: 68.4 us; the launch traced here: 68.2 us
  Pallas kernels  64.9 us (95%)
  local copies, waits for them, and re-layouts  2.62 us (4%)
    pallas_call x1, Pallas kernels, local(): pl.pallas_call(functools.partial(kernel, ORDER), name='probes', out_shape...  64.9 us
    unnamed x2, local copies, waits for them, and re-layouts  2.62 us

profile of v2, /device:TPU:0, one launch (start us, length us, event | category | flops | bytes accessed | tf_op | source)
XLA Modules:
  0.0 68.2 jit_solution(11452382549597218899)
XLA Ops:
  0.6 64.9 %probes.1 = (f32[4,2048]{1,0:T(4,128)}, f32[4,4]{1,0:T(4,128)}) custom-call(f32[512,2048]{1,0:T(8,128)} %green.1, f32[2048,512]{1,0:T(8,128)} %field.1, f32[4,2048]{1,0:T(4,128)} %probe.1, f32[512,1024]{1,0:T(8,128)} %cov.1), custom_call_target="tpu_custom_call" | custom-call | flops 25769803776 | bytes 10485760 | tf_op jit(solution)/shard_map/probes/pallas_call | solution.py:265
  65.5 1.4 %copy.8 = f32[4,2048]{1,0:T(4,128)} copy(f32[4,2048]{1,0:T(4,128)} %get-tuple-element.4) | data formatting | bytes 65536
  66.9 1.2 %copy.9 = f32[4,4]{1,0:T(4,128)} copy(f32[4,4]{1,0:T(4,128)} %get-tuple-element.5) | data formatting | bytes 128

commit v3 on v2

--- a/solution.py
+++ b/solution.py
@@ -20,11 +20,11 @@
 NNB = C // NB
 
 ORDER = [
-    "F1a.0", "F1b.0", "F0a.0", "F0b.0", "F1a.1", "C.0", "F1b.1", "F0a.1", "F0b.1", "F1a.2", "C.1", "F1b.2",
-    "F0a.2", "F0b.2", "A.0", "F1a.3", "C.2", "F1b.3", "F0a.3", "F0b.3", "A.1", "C.3", "R.0", "A.2", "R.1",
-    "A.3", "V.0", "R.2", "V.1", "U.0", "B0a.0", "R.3", "V.2", "B0b.0", "G0", "U.1", "B1a.0", "B1b.0",
-    "B0a.1", "V.3", "B0b.1", "B1a.1", "U.2", "B1b.1", "G1", "B0a.2", "B0b.2", "B1a.2", "U.3", "B1b.2",
-    "B0a.3", "B0b.3", "G2", "B1a.3", "B1b.3", "G3",
+    "P.0", "P.1", "F1a.0", "P.2", "P.3", "F1b.0", "F0a.0", "F0b.0", "F1a.1", "C.0", "F1b.1", "F0a.1",
+    "F0b.1", "F1a.2", "C.1", "F1b.2", "F0a.2", "A.0", "F0b.2", "F1a.3", "C.2", "F1b.3", "A.1", "F0a.3",
+    "F0b.3", "C.3", "R.0", "A.2", "R.1", "V.0", "A.3", "R.2", "V.1", "U.0", "B0a.0", "B0b.0", "R.3", "V.2",
+    "G0", "B1a.0", "U.1", "B1b.0", "B0a.1", "V.3", "B0b.1", "B1a.1", "U.2", "G1", "B1b.1", "B0a.2", "B0b.2",
+    "U.3", "B1a.2", "B1b.2", "G2", "B0a.3", "B0b.3", "B1a.3", "B1b.3", "G3",
 ]
 
 
@@ -51,9 +51,9 @@
     return lax.dot_general(a, b, (((1,), (0,)), ((), ())), preferred_element_type=F32)
 
 
-def kernel(order, green, field, probe, cov, h_out, g_out,
+def kernel(order, green, field, probe, cov, h_out, away_out, g_out,
            graw, fraw, craw, prb, ghi, glo, ft, chi, clo, data, core_in, ring_in, pair_in, own, white, hess, hess_in,
-           gram, g8, g4, g2, g1, lsem, ssem, rsem):
+           gram, g16, g4, g2, g1, lsem, ssem, rsem):
     cell = lax.axis_index("cell")
     rcv = lax.axis_index("rcv")
     core = lax.rem(cell, 2)
@@ -111,7 +111,8 @@
     place_c = [core, 1 - core]
 
     load_probe.wait()
-    for k in range(NKB):
+
+    def prepare(k):
         cells = slice(k * KB, (k + 1) * KB)
         loads[2 * k].wait()
         turned = fraw[cells, :].T
@@ -174,7 +175,9 @@
     for word in order:
         op, _, p = word.partition(".")
         p = int(p) if p else 0
-        if op == "F1a":
+        if op == "P":
+            prepare(p)
+        elif op == "F1a":
             forward(p, 1, 0)
         elif op == "F1b":
             forward(p, 1, 1)
@@ -222,38 +225,36 @@
             backward(p, 1, 0)
         elif op == "B1b":
             backward(p, 1, 1)
+            h_out[p:p + 1, :] = hess[p]
             waits["H", p] = remote(hess.at[p], hess_in.at[p], other)
         elif op == "G0":
             for a in range(NP):
                 for b in range(NP):
                     t = jnp.sum(own[a] * white[b, 0:8], axis=0, keepdims=True)
                     gram[a * NP + b:a * NP + b + 1, :] = (t[:, 0:128] + t[:, 128:256]) + (t[:, 256:384] + t[:, 384:])
-            waits["G"] = [remote(gram, g8.at[m - 1], pairs[m]) for m in range(1, 8)]
+            waits["G"] = [remote(gram, g16.at[n], dev) for n, dev in enumerate(facing + pairs[1:])]
         elif op == "G1":
             for c in waits["G"]:
                 c.wait_recv()
             total = gram[...]
-            for m in range(7):
-                total += g8[m]
+            for m in range(15):
+                total += g16[m]
             g1[0] = total
             waits["G"] = [remote(g1.at[0], g4.at[m - 1], ring[m]) for m in (1, 2, 3)]
         elif op == "G2":
             for c in waits["G"]:
                 c.wait_recv()
             g1[1] = (g1[0] + g4[0]) + (g4[1] + g4[2])
-            waits["G"] = [remote(g1.at[1], g2.at[0], sibling)]
+            waits["G"] = [remote(g1.at[1], g2, sibling)]
         elif op == "G3":
             waits["G"][0].wait_recv()
-            g1[2] = g1[1] + g2[0]
-            waits["G"] = [remote(g1.at[2], g2.at[1], other)]
+            sums = jnp.sum(g1[1] + g2[...], axis=1, keepdims=True)
+            for a in range(NP):
+                for b in range(NP):
+                    g_out[a:a + 1, b:b + 1] = sums[a * NP + b:a * NP + b + 1, :]
     for p in range(NP):
         waits["H", p].wait_recv()
-        h_out[p:p + 1, :] = hess[p] + hess_in[p]
-    waits["G"][0].wait_recv()
-    sums = jnp.sum(g1[2] + g2[1], axis=1, keepdims=True) * (1.0 / (2 * R * S))
-    for a in range(NP):
-        for b in range(NP):
-            g_out[a:a + 1, b:b + 1] = sums[a * NP + b:a * NP + b + 1, :]
+        away_out[p:p + 1, :] = hess_in[p]
     for c in started:
         c.wait_send()
 
@@ -261,13 +262,14 @@
 def local(green, field, probe, cov):
     any_spec = pl.BlockSpec(memory_space=pl.ANY)
     vmem = pl.BlockSpec(memory_space=pltpu.VMEM)
-    n_remote = NP * 32 + 12
-    return pl.pallas_call(
+    n_remote = NP * 32 + 20
+    mine, away, sums = pl.pallas_call(
         functools.partial(kernel, ORDER),
         name="probes",
-        out_shape=(jax.ShapeDtypeStruct((NP, C), F32), jax.ShapeDtypeStruct((NP, NP), F32)),
+        out_shape=(jax.ShapeDtypeStruct((NP, C), F32), jax.ShapeDtypeStruct((NP, C), F32),
+                   jax.ShapeDtypeStruct((NP, NP), F32)),
         in_specs=[any_spec] * 4,
-        out_specs=(vmem, vmem),
+        out_specs=(vmem, vmem, vmem),
         scratch_shapes=[
             pltpu.VMEM((R, C), F32),
             pltpu.VMEM((C, S), F32),
@@ -287,10 +289,10 @@
             pltpu.VMEM((NP, 1, C), F32),
             pltpu.VMEM((NP, 1, C), F32),
             pltpu.VMEM((16, 128), F32),
-            pltpu.VMEM((7, 16, 128), F32),
+            pltpu.VMEM((15, 16, 128), F32),
             pltpu.VMEM((3, 16, 128), F32),
+            pltpu.VMEM((16, 128), F32),
             pltpu.VMEM((2, 16, 128), F32),
-            pltpu.VMEM((3, 16, 128), F32),
             pltpu.SemaphoreType.DMA((2 * NKB + 2,)),
             pltpu.SemaphoreType.DMA((n_remote,)),
             pltpu.SemaphoreType.DMA((n_remote,)),
@@ -298,6 +300,7 @@
         compiler_params=pltpu.CompilerParams(collective_id=0, has_side_effects=True, vmem_limit_bytes=56 * 2 ** 20),
         cost_estimate=pl.CostEstimate(flops=6 * 2 * R * C * S * NP, bytes_accessed=10 * 2 ** 20, transcendentals=0),
     )(green, field, probe, cov)
+    return mine + away, sums / (2 * R * S)
 
 
 def solution(mesh):

time: 68.4 us -> 67.6 us (0.988)
  other arithmetic: 0 us -> 2.64 us
  local copies, waits for them, and re-layouts: 2.62 us -> 0 us
  Pallas kernels: 64.9 us -> 64.1 us
    unnamed x2 -> x0, local copies, waits for them, and re-layouts: 2.62 us -> none
    add x0 -> x1, other arithmetic: none -> 1.4 us  [local(): return (mine + away, sums / (2 * R * S))]
    div x0 -> x1, other arithmetic: none -> 1.24 us  [local(): return (mine + away, sums / (2 * R * S))]
    pallas_call x1, Pallas kernels: 64.9 us -> 64.1 us  [local(): pl.pallas_call(functools.partial(kernel, ORDER), name='probes', out_shape...]
where the time goes in v3:
time: 67.6 us; the launch traced here: 67.4 us
  Pallas kernels  64.1 us (95%)
  other arithmetic  2.64 us (4%)
    pallas_call x1, Pallas kernels, local(): pl.pallas_call(functools.partial(kernel, ORDER), name='probes', out_shape...  64.1 us
    add x1, other arithmetic, local(): return (mine + away, sums / (2 * R * S))  1.4 us

profile of v3, /device:TPU:0, one launch (start us, length us, event | category | flops | bytes accessed | tf_op | source)
XLA Modules:
  0.0 67.4 jit_solution(6625264325682865415)
XLA Ops:
  0.6 64.1 %probes.1 = (f32[4,2048]{1,0:T(4,128)}, f32[4,2048]{1,0:T(4,128)}, f32[4,4]{1,0:T(4,128)}) custom-call(f32[512,2048]{1,0:T(8,128)} %green.1, f32[2048,512]{1,0:T(8,128)} %field.1, f32[4,2048]{1,0:T(4,128)} %probe.1, f32[512,1024]{1,0:T(8,128)} %cov.1), custom_call_target="tpu_custom_call" | custom-call | flops 25769803776 | bytes 10485760 | tf_op jit(solution)/shard_map/probes/pallas_call | solution.py:266
  64.7 1.4 %add.3 = f32[4,2048]{1,0:T(4,128)} add(f32[4,2048]{1,0:T(4,128)} %get-tuple-element.5, f32[4,2048]{1,0:T(4,128)} %get-tuple-element.6) | non-fusion elementwise | flops 8192 | bytes 98304 | tf_op jit(solution)/shard_map/add | solution.py:303
  66.1 1.2 %broadcast_multiply_fusion = f32[4,4]{1,0:T(4,128)} fusion(f32[4,4]{1,0:T(4,128)} %get-tuple-element.7), kind=kLoop, calls=%fused_computation | loop fusion | flops 16 | bytes 128 | tf_op jit(solution)/shard_map/div | solution.py:303

commit v4 on v3

--- a/solution.py
+++ b/solution.py
@@ -21,9 +21,9 @@
 
 ORDER = [
     "P.0", "P.1", "F1a.0", "P.2", "P.3", "F1b.0", "F0a.0", "F0b.0", "F1a.1", "C.0", "F1b.1", "F0a.1",
-    "F0b.1", "F1a.2", "C.1", "F1b.2", "F0a.2", "A.0", "F0b.2", "F1a.3", "C.2", "F1b.3", "A.1", "F0a.3",
-    "F0b.3", "C.3", "R.0", "A.2", "R.1", "V.0", "A.3", "R.2", "V.1", "U.0", "B0a.0", "B0b.0", "R.3", "V.2",
-    "G0", "B1a.0", "U.1", "B1b.0", "B0a.1", "V.3", "B0b.1", "B1a.1", "U.2", "G1", "B1b.1", "B0a.2", "B0b.2",
+    "F0b.1", "F1a.2", "C.1", "F1b.2", "A.0", "F0a.2", "F0b.2", "F1a.3", "C.2", "F1b.3", "A.1", "F0a.3",
+    "F0b.3", "R.0", "C.3", "A.2", "R.1", "V.0", "A.3", "R.2", "V.1", "U.0", "B0a.0", "B0b.0", "R.3", "V.2",
+    "G0", "U.1", "B1a.0", "B1b.0", "B0a.1", "V.3", "B0b.1", "B1a.1", "U.2", "G1", "B1b.1", "B0a.2", "B0b.2",
     "U.3", "B1a.2", "B1b.2", "G2", "B0a.3", "B0b.3", "B1a.3", "B1b.3", "G3",
 ]
 

time: 67.6 us -> 68.8 us (1.018)
  Pallas kernels: 64.1 us -> 65.3 us
    pallas_call x1, Pallas kernels: 64.1 us -> 65.3 us  [local(): pl.pallas_call(functools.partial(kernel, ORDER), name='probes', out_shape...]
where the time goes in v4:
time: 68.8 us; the launch traced here: 68.6 us
  Pallas kernels  65.3 us (95%)
  other arithmetic  2.64 us (4%)
    pallas_call x1, Pallas kernels, local(): pl.pallas_call(functools.partial(kernel, ORDER), name='probes', out_shape...  65.3 us
    add x1, other arithmetic, local(): return (mine + away, sums / (2 * R * S))  1.4 us

profile of v4, /device:TPU:0, one launch (start us, length us, event | category | flops | bytes accessed | tf_op | source)
XLA Modules:
  0.0 68.6 jit_solution(18194518129404217340)
XLA Ops:
  0.6 65.3 %probes.1 = (f32[4,2048]{1,0:T(4,128)}, f32[4,2048]{1,0:T(4,128)}, f32[4,4]{1,0:T(4,128)}) custom-call(f32[512,2048]{1,0:T(8,128)} %green.1, f32[2048,512]{1,0:T(8,128)} %field.1, f32[4,2048]{1,0:T(4,128)} %probe.1, f32[512,1024]{1,0:T(8,128)} %cov.1), custom_call_target="tpu_custom_call" | custom-call | flops 25769803776 | bytes 10485760 | tf_op jit(solution)/shard_map/probes/pallas_call | solution.py:266
  65.9 1.4 %add.3 = f32[4,2048]{1,0:T(4,128)} add(f32[4,2048]{1,0:T(4,128)} %get-tuple-element.5, f32[4,2048]{1,0:T(4,128)} %get-tuple-element.6) | non-fusion elementwise | flops 8192 | bytes 98304 | tf_op jit(solution)/shard_map/add | solution.py:303
  67.3 1.2 %broadcast_multiply_fusion = f32[4,4]{1,0:T(4,128)} fusion(f32[4,4]{1,0:T(4,128)} %get-tuple-element.7), kind=kLoop, calls=%fused_computation | loop fusion | flops 16 | bytes 128 | tf_op jit(solution)/shard_map/div | solution.py:303
